TPU v7x, 32 devices: a whole 2x2x4 slice. The times are simulated.
32 devices in a mesh: chrom: 4 (over y, x), snp: 8 (over z, core).
Axes of the slice: x: 2, y: 2, z: 4, core: 2. Of those that a mesh axis runs over, the one named last changes fastest.
Arguments:
- genotypes: bfloat16 [12288, 16384], P(None, ('chrom', 'snp')), may hold values from 0 to 2, as said below
- probes: bfloat16 [16384, 128], P(('chrom', 'snp')), may hold values from -4 to 4
Outputs:
- unit_basis: float32 [16384, 128], P(('chrom', 'snp'))
- range_log_norms: float32 [128], replicated
Inputs may be any that keep to these rules, and one draw needn't show every extreme that they name: `genotypes`: every entry is a dosage 0, 1 or 2.
All inputs are finite; a program needn't handle non-finite values.
Results may differ from a plain program's by a relative error of at most 0.0034.
The roundings to bfloat16 on the way count: a program that leaves them out, or rounds other values in their place, can miss the bound.
Values sent between devices are 32-bit elements; how exact they have to be, the bound alone decides.
A program may use at most 128 MiB of HBM per device.

v0:
```python
import math

import jax
import jax.numpy as jnp
from jax import lax
from jax.sharding import PartitionSpec as P


def standardize(block):
    values = block.astype(jnp.float32)
    column_mean = jnp.mean(values, axis=0, keepdims=True)
    centered = values - column_mean
    spread = jnp.mean(centered * centered, axis=0, keepdims=True)
    return (centered * (spread + 1e-05) ** (-0.125)).astype(jnp.bfloat16)


def split_parts(sketch):
    sketch_high = lax.optimization_barrier(sketch.astype(jnp.bfloat16))
    remainder = sketch - sketch_high.astype(jnp.float32)
    sketch_mid = lax.optimization_barrier(remainder.astype(jnp.bfloat16))
    sketch_low = (remainder - sketch_mid.astype(jnp.float32)).astype(jnp.bfloat16)
    return jnp.concatenate([sketch_high, sketch_mid, sketch_low], axis=1)


def column_gram(matrix):
    return lax.dot_general(
        matrix,
        matrix,
        (((0,), (0,)), ((), ())),
        precision=lax.Precision.HIGHEST,
        preferred_element_type=jnp.float32,
    )


def unit_columns(matrix, gram_matrix):
    lower_factor = jnp.linalg.cholesky(gram_matrix)
    return lax.linalg.triangular_solve(
        lower_factor, matrix, left_side=False, lower=True, transpose_a=True
    )


def body(genotypes, probes):
    scaled = standardize(genotypes)
    width = probes.shape[1]
    partial_sketch = jnp.dot(scaled, probes, preferred_element_type=jnp.float32)
    sketch = lax.psum(partial_sketch, ("chrom", "snp"))
    sketch_parts = split_parts(sketch)
    product = lax.dot_general(
        scaled, sketch_parts, (((0,), (0,)), ((), ())), preferred_element_type=jnp.float32
    )
    range_rows = product[:, :width] + product[:, width : 2 * width] + product[:, 2 * width :]
    total_snps = range_rows.shape[0] * lax.axis_size("chrom") * lax.axis_size("snp")
    gram_first = lax.psum(column_gram(range_rows), ("chrom", "snp"))
    range_log_norms = 0.1 * jnp.log(jnp.diagonal(gram_first) / total_snps)
    first_basis = unit_columns(range_rows, gram_first)
    gram_second = lax.psum(column_gram(first_basis), ("chrom", "snp"))
    second_basis = unit_columns(first_basis, gram_second)
    return (second_basis * math.sqrt(total_snps), range_log_norms)


def solution(mesh):
    return jax.shard_map(
        body,
        mesh=mesh,
        in_specs=(P(None, ("chrom", "snp")), P(("chrom", "snp"), None)),
        out_specs=(P(("chrom", "snp"), None), P()),
        check_vma=False,
    )
```

profile of v0, /device:TPU:0, one launch (start us, length us, event | category | flops | bytes accessed | tf_op | source)
XLA Modules:
  0.0 497.1 jit_solution(3341795115427126927)
XLA Ops:
  7.2 0.0 copy-start
  7.2 0.0 all-reduce.4.cloned.1.call-start
  7.2 0.0 copy-start.2
  7.2 7.9 %convert_reduce_fusion = f32[512]{0:T(512)S(1)} fusion(bf16[12288,512]{1,0:T(8,128)(2,1)} %param.5), kind=kLoop, calls=%fused_computation.2 | loop fusion | flops 12582400 | bytes 12584960 | tf_op jit(solution)/shard_map/reduce_sum | solution.py:11
  15.2 0.4 copy-done.2
  15.6 3.6 fusion.2
  19.2 0.0 copy-done
  19.2 5.3 %fusion.6 = f32[12288,128]{1,0:T(8,128)} fusion(bf16[512,128]{1,0:T(8,128)(2,1)S(1)} %copy-done, bf16[12288,512]{1,0:T(8,128)(2,1)S(1)} %copy-done.2, f32[512]{0:T(512)S(1)} %add_power_fusion, f32[512]{0:T(512)S(1)} %broadcast_multiply_fusion), kind=kOutput, calls=%fused_computation.8 | convolution fusion | flops 1635778560 | bytes 19009536 | tf_op jit(solution)/shard_map/dot_general | solution.py:45
  24.5 0.0 all-reduce.4.cloned.1.call-update
  24.5 0.0 all-reduce.6.cloned.1.call-start
  24.6 158.7 %all-reduce.4.cloned.1.call-done = f32[12288,128]{1,0:T(8,128)} async-done(((f32[12288,128]{1,0:T(8,128)}), f32[12288,128]{1,0:T(8,128)}) %all-reduce.4.cloned.1.call-update) | async-done | bytes 6291472 | tf_op jit(solution)/shard_map/psum | solution.py:46
  183.3 0.0 copy-start.1
  183.3 3.2 convert_element_type.23
  186.4 1.5 copy-done.1
  187.9 0.8 fusion.13
  188.7 1.3 subtract_convert_fusion
  190.0 11.3 %fusion.4 = f32[512,384]{1,0:T(8,128)S(1)} fusion(bf16[12288,512]{1,0:T(8,128)(2,1)} %param.5, f32[512]{0:T(512)S(1)} %add_power_fusion, f32[512]{0:T(512)S(1)} %broadcast_multiply_fusion, bf16[12288,128]{1,0:T(8,128)(2,1)S(1)} %subtract_convert_fusion, bf16[12288,128]{1,0:T(8,128)(2,1)S(1)} %fusion.13, bf16[12288,128]{1,0:T(8,128)(2,1)S(1)} %convert_element_type.23), kind=kOutput, calls=%fused_computation.7 | convolution fusion | flops 4885315584 | bytes 22810624 | tf_op jit(solution)/shard_map/dot_general | solution.py:48
  201.4 1.2 fusion.24
  202.6 0.0 all-reduce.6.cloned.1.call-update
  202.6 0.2 all-reduce.8.cloned.1.call-start
  202.9 117.2 %all-reduce.6.cloned.1.call-done = f32[128,128]{0,1:T(8,128)} async-done(((f32[128,128]{0,1:T(8,128)}), f32[128,128]{0,1:T(8,128)}) %all-reduce.6.cloned.1.call-update) | async-done | bytes 65552 | tf_op jit(solution)/shard_map/psum | solution.py:53
  320.0 0.9 copy.10
  321.0 0.9 fusion.20
  321.8 11.7 %cholesky.44 = f32[128,128]{1,0:T(8,128)S(1)} custom-call(f32[128,128]{1,0:T(8,128)S(1)} %fusion.20), custom_call_target="Cholesky" | custom-call | tf_op jit(solution)/shard_map/jit(cholesky)/cholesky | solution.py:36
  333.6 0.6 compare_reduce_fusion.1
  334.2 0.7 fusion.15
  334.9 9.8 %custom-call.8 = f32[1,128,128]{1,2,0:T(8,128)S(1)} custom-call(f32[1,128,128]{2,1,0:T(8,128)S(1)} %fusion.15), custom_call_target="InvertDiagBlocksLowerTriangular" | custom-call | tf_op jit(solution)/shard_map/triangular_solve/custom-call.0 | solution.py:37
  344.7 0.4 convolution_bitcast_fusion.1
  345.1 1.0 fusion.25
  346.1 0.0 all-reduce.8.cloned.1.call-update
  346.2 1.9 gather_fusion
  348.1 0.5 log_multiply_fusion
  348.6 116.1 %all-reduce.8.cloned.1.call-done = f32[128,128]{0,1:T(8,128)} async-done(((f32[128,128]{0,1:T(8,128)}), f32[128,128]{0,1:T(8,128)}) %all-reduce.8.cloned.1.call-update) | async-done | bytes 65552 | tf_op jit(solution)/shard_map/psum | solution.py:56
  464.7 0.9 copy.12
  465.6 0.9 fusion.18
  466.5 11.7 %cholesky.55 = f32[128,128]{1,0:T(8,128)S(1)} custom-call(f32[128,128]{1,0:T(8,128)S(1)} %fusion.18), custom_call_target="Cholesky" | custom-call | tf_op jit(solution)/shard_map/jit(cholesky)/cholesky | solution.py:36
  478.2 0.6 compare_reduce_fusion
  478.9 0.7 fusion.16
  479.5 9.8 %custom-call.9 = f32[1,128,128]{1,2,0:T(8,128)S(1)} custom-call(f32[1,128,128]{2,1,0:T(8,128)S(1)} %fusion.16), custom_call_target="InvertDiagBlocksLowerTriangular" | custom-call | tf_op jit(solution)/shard_map/triangular_solve/custom-call.0 | solution.py:37
  489.3 0.4 fusion.14
  489.8 0.8 copy.13
  (5 shorter events, 0.1 us)
Async XLA Ops:
  7.2 12.0 %copy-start = (bf16[512,128]{1,0:T(8,128)(2,1)S(1)}, bf16[512,128]{1,0:T(8,128)(2,1)}, u32[]{:S(2)}) copy-start(bf16[512,128]{1,0:T(8,128)(2,1)} %param.6) | copy-start | bytes 393220
  7.2 176.1 %all-reduce.4.cloned.1.call-start = ((), (), s32[]{:S(2)}) async-start(), calls=%async_computation | async-start | bytes 12582912 | tf_op jit(solution)/shard_map/psum | solution.py:46
  7.2 8.4 %copy-start.2 = (bf16[12288,512]{1,0:T(8,128)(2,1)S(1)}, bf16[12288,512]{1,0:T(8,128)(2,1)}, u32[]{:S(2)}) copy-start(bf16[12288,512]{1,0:T(8,128)(2,1)} %param.5) | copy-start | bytes 37748740
  24.5 295.5 %all-reduce.6.cloned.1.call-start = ((), (), s32[]{:S(2)}) async-start(), calls=%async_computation.1 | async-start | bytes 131072 | tf_op jit(solution)/shard_map/psum | solution.py:53
  183.3 4.6 copy-start.1
  202.6 262.1 %all-reduce.8.cloned.1.call-start = ((), (), s32[]{:S(2)}) async-start(), calls=%async_computation.2 | async-start | bytes 131072 | tf_op jit(solution)/shard_map/psum | solution.py:56
Sparse Core Ops, SparseCore 0:
  24.6 158.5 all-reduce.3
  202.7 117.2 all-reduce.5
  346.3 118.3 all-reduce.7
where the time goes:
time: 499 us; the launch traced here: 497 us
  waiting for transfers between devices  392 us (79%)
  other arithmetic  64.7 us (13%)
  matrix products  19.7 us (4%)
  between operations  13.9 us (3%)
  local copies, waits for them, and re-layouts  6.55 us (1%)
    psum x1, waiting for transfers between devices, body(): sketch = lax.psum(partial_sketch, ('chrom', 'snp'))  159 us
    psum x1, waiting for transfers between devices, body(): gram_first = lax.psum(column_gram(range_rows), ('chrom', 'snp'))  117 us
    psum x1, waiting for transfers between devices, body(): gram_second = lax.psum(column_gram(first_basis), ('chrom', 'snp'))  116 us
    another operation x6, other arithmetic, unit_columns(): lower_factor = jnp.linalg.cholesky(gram_matrix)  24.8 us
    another operation x4, other arithmetic, unit_columns(): lax.linalg.triangular_solve(lower_factor, matrix, left_side=False, lower=...  20.9 us
    dot_general x1, matrix products, body(): lax.dot_general(scaled, sketch_parts, (((0,), (0,)), ((), ())), preferred...  11.3 us
  transfers between devices with their start and end apart: 3, of which 3 were waited for; matrix products, arithmetic and copies ran while one was open for 0% of the time, Pallas kernels for 0%

commit v1 on v0

v1 whole, which is shorter than its diff:
```python
import functools
import math

import jax
import jax.numpy as jnp
from jax import lax
from jax.experimental import pallas as pl
from jax.experimental.pallas import tpu as pltpu
from jax.sharding import PartitionSpec as P

MESH = pl.DeviceIdType.MESH
AXES = ("chrom", "snp")
HIGHEST = lax.Precision.HIGHEST
F32 = jnp.float32
BF16 = jnp.bfloat16


def split_size(size):
    factors = []
    while size > 1:
        factor = 4 if size % 4 == 0 and size > 2 else 2 if size % 2 == 0 else size
        factors.append(factor)
        size //= factor
    return factors


def axis_factors(axis, sizes):
    out, stride = [], 1
    for size in reversed(sizes):
        out.append((axis, stride, size))
        stride *= size
    return out[::-1]


def mesh_factors(chroms, snps):
    halves, rest = [], chroms
    while rest % 2 == 0:
        halves.append(2)
        rest //= 2
    if rest > 1:
        halves.append(rest)
    chrom = axis_factors("chrom", halves)
    core = 2 if snps % 2 == 0 else 1
    snp = [(a, s * core, n) for a, s, n in axis_factors("snp", split_size(snps // core))]
    cores = [("snp", 1, core)] if core > 1 else []
    return cores, chrom, snp


def coordinate(factor):
    axis, stride, size = factor
    return lax.rem(lax.div(lax.axis_index(axis), stride), size)


def peer_id(factor, distance):
    axis, stride, size = factor
    mine = coordinate(factor)
    other = lax.rem(mine + distance, size)
    return tuple(
        lax.axis_index(a) + (other - mine) * stride if a == axis else lax.axis_index(a)
        for a in AXES
    )


def greet(factors):
    barrier = pltpu.get_barrier_semaphore()
    count = 0
    for factor in factors:
        for distance in range(1, factor[2]):
            pl.semaphore_signal(
                barrier, inc=1, device_id=peer_id(factor, distance), device_id_type=MESH
            )
            count += 1
    pl.semaphore_wait(barrier, count)


def rows_of(start, rows):
    return pl.ds(pl.multiple_of(start, 8), rows)


def block_of(rows, most):
    return max(b for b in range(8, most + 1, 8) if rows % b == 0)


class Plan:
    def __init__(self, samples, chroms, snps):
        self.devices = chroms * snps
        per_device = samples // self.devices
        self.pieces = next(q for q in (8, 6, 4, 3, 2, 1) if per_device % (8 * q) == 0)
        self.rows = samples // self.pieces
        self.cores, self.chrom, self.snp = mesh_factors(chroms, snps)
        self.factors = self.cores + self.chrom + self.snp
        self.slots = sum(f[2] - 1 for f in self.factors)

    def order(self, piece):
        turn = piece % max(1, len(self.chrom))
        return self.cores + self.chrom[turn:] + self.chrom[:turn] + self.snp

    def received(self):
        return self.rows


def range_kernel(plan, geno_hbm, probes_ref, range_ref, gram_ref, values, part, full, recv, acc, load_sem, rs_send, rs_recv, ag_send, ag_recv):
    samples, snps = values.shape
    width = probes_ref.shape[1]
    rows, pieces = plan.rows, plan.pieces
    loads = []
    for q in range(pieces):
        piece = pl.ds(q * rows, rows)
        load = pltpu.make_async_copy(geno_hbm.at[piece], values.at[piece], load_sem.at[q])
        load.start()
        loads.append(load)
    greet(plan.factors)

    block = math.gcd(rows, 512)
    zero = jnp.zeros((16, snps), F32)
    sums = (zero, zero)
    for q in range(pieces):
        loads[q].wait()

        def add_block(i, carry, q=q):
            first, second = carry
            start = q * rows + i * block
            one = jnp.zeros((16, snps), BF16)
            two = jnp.zeros((16, snps), BF16)
            for slab in range(block // 16):
                x = values[pl.ds(pl.multiple_of(start + slab * 16, 16), 16), :]
                one = one + x
                two = two + x * x
            return first + one.astype(F32), second + two.astype(F32)

        sums = lax.fori_loop(0, rows // block, add_block, sums)
    total = jnp.sum(sums[0], axis=0, keepdims=True)
    squares = jnp.sum(sums[1], axis=0, keepdims=True)
    mean = total / samples
    whole, square = total.astype(jnp.int32), squares.astype(jnp.int32)
    spread = (square * samples - whole * whole).astype(F32) / float(samples) ** 2
    factor = lax.rsqrt(jnp.sqrt(jnp.sqrt(spread + 1e-05)))
    probes = probes_ref[...]
    acc[...] = jnp.zeros_like(acc)

    tile = math.gcd(rows, 256)

    def sketch_piece(q):
        def one_tile(i, _):
            at = pl.ds(pl.multiple_of(q * rows + i * tile, 16), tile)
            scaled = ((values[at, :].astype(F32) - mean) * factor).astype(BF16)
            values[at, :] = scaled
            part[at, :] = jnp.dot(scaled, probes, preferred_element_type=F32)
            return 0

        lax.fori_loop(0, rows // tile, one_tile, 0)

    bases = []
    for q in range(pieces):
        base, size, path = q * rows, rows, []
        slot, offset = 0, 0
        for factor_ in plan.order(q):
            share = size // factor_[2]
            path.append((factor_, base, share, slot, offset))
            slot += factor_[2] - 1
            offset += (factor_[2] - 1) * share
            base = base + coordinate(factor_) * share
            size = share
        path.append((None, base, size, slot, offset))
        bases.append(path)
    stages = len(plan.factors)
    copies = {}

    def scatter_start(q, s):
        factor_, base, share, slot, offset = bases[q][s]
        sent = []
        for distance in range(1, factor_[2]):
            other = lax.rem(coordinate(factor_) + distance, factor_[2])
            copy = pltpu.make_async_remote_copy(
                src_ref=part.at[rows_of(base + other * share, share)],
                dst_ref=recv.at[q, pl.ds(offset + (distance - 1) * share, share)],
                send_sem=rs_send.at[q, slot + distance - 1],
                recv_sem=rs_recv.at[q, slot + distance - 1],
                device_id=peer_id(factor_, distance),
                device_id_type=MESH,
            )
            copy.start()
            sent.append(copy)
        copies["rs", q, s] = sent

    def scatter_end(q, s):
        factor_, _, share, _, offset = bases[q][s]
        base = bases[q][s + 1][1]
        for copy in copies["rs", q, s]:
            copy.wait_recv()
        step = block_of(share, 64)
        last = s == stages - 1

        def add(i, _):
            at = rows_of(base + i * step, step)
            value = part[at, :]
            for k in range(factor_[2] - 1):
                value = value + recv[q, rows_of(offset + k * share + i * step, step), :]
            if last:
                full[at, :] = value
            else:
                part[at, :] = value
            return 0

        lax.fori_loop(0, share // step, add, 0)

    def gather_start(q, s):
        factor_, _, share, slot, _ = bases[q][s]
        at = rows_of(bases[q][s + 1][1], share)
        sent = []
        for distance in range(1, factor_[2]):
            copy = pltpu.make_async_remote_copy(
                src_ref=full.at[at],
                dst_ref=full.at[at],
                send_sem=ag_send.at[q, slot + distance - 1],
                recv_sem=ag_recv.at[q, slot + distance - 1],
                device_id=peer_id(factor_, distance),
                device_id_type=MESH,
            )
            copy.start()
            sent.append(copy)
        copies["ag", q, s] = sent

    def gather_end(q, s):
        for copy in copies["ag", q, s]:
            copy.wait_recv()

    depth = math.gcd(rows, 768)

    def project(q):
        def one(i, _):
            at = pl.ds(pl.multiple_of(q * rows + i * depth, 16), depth)
            sketch = full[at, :].T
            high = sketch.astype(BF16)
            rest = sketch - high.astype(F32)
            mid = rest.astype(BF16)
            low = (rest - mid.astype(F32)).astype(BF16)
            parts = jnp.concatenate([high, mid, low], axis=0)
            acc[...] += jnp.dot(parts, values[at, :], preferred_element_type=F32)
            return 0

        lax.fori_loop(0, rows // depth, one, 0)

    def step(q, t):
        if t == 0:
            sketch_piece(q)
            if stages:
                scatter_start(q, 0)
            else:
                full[pl.ds(q * rows, rows), :] = part[pl.ds(q * rows, rows), :]
        elif t < stages:
            scatter_end(q, t - 1)
            scatter_start(q, t)
        elif t == stages:
            scatter_end(q, t - 1)
            gather_start(q, stages - 1)
        elif t < 2 * stages:
            gather_end(q, 2 * stages - t)
            gather_start(q, 2 * stages - t - 1)
        else:
            gather_end(q, 0)
            project(q)

    for time in range(pieces + 2 * stages):
        for q in range(pieces):
            if 0 <= time - q <= 2 * stages:
                step(q, time - q)
    for sent in copies.values():
        for copy in sent:
            copy.wait_send()

    result = acc[:width] + acc[width : 2 * width] + acc[2 * width :]
    range_ref[...] = result
    gram_ref[...] = lax.dot_general(
        result, result, (((1,), (1,)), ((), ())), precision=HIGHEST, preferred_element_type=F32
    )


def range_rows(plan, genotypes, probes):
    samples, snps = genotypes.shape
    width = probes.shape[1]
    slots = max(1, plan.slots)
    return pl.pallas_call(
        functools.partial(range_kernel, plan),
        out_shape=(
            jax.ShapeDtypeStruct((width, snps), F32),
            jax.ShapeDtypeStruct((width, width), F32),
        ),
        in_specs=[pl.BlockSpec(memory_space=pl.ANY), pl.BlockSpec(memory_space=pltpu.VMEM)],
        out_specs=[pl.BlockSpec(memory_space=pltpu.VMEM)] * 2,
        scratch_shapes=[
            pltpu.VMEM((samples, snps), BF16),
            pltpu.VMEM((samples, width), F32),
            pltpu.VMEM((samples, width), F32),
            pltpu.VMEM((plan.pieces, plan.rows, width), F32),
            pltpu.VMEM((3 * width, snps), F32),
            pltpu.SemaphoreType.DMA((plan.pieces,)),
            pltpu.SemaphoreType.DMA((plan.pieces, slots)),
            pltpu.SemaphoreType.DMA((plan.pieces, slots)),
            pltpu.SemaphoreType.DMA((plan.pieces, slots)),
            pltpu.SemaphoreType.DMA((plan.pieces, slots)),
        ],
        compiler_params=pltpu.CompilerParams(
            collective_id=0, has_side_effects=True, vmem_limit_bytes=48 * 1024 * 1024
        ),
        name="range_rows",
    )(genotypes, probes)


def basis_kernel(last, gram_ref, rows_ref, out_ref, gram_out_ref, work):
    width = gram_ref.shape[0]
    row = lax.broadcasted_iota(jnp.int32, (width, width), 0)
    lane = lax.broadcasted_iota(jnp.int32, (width, width), 1)
    work[:, :width] = gram_ref[...]
    work[:, width:] = jnp.where(row == lane, 1.0, 0.0).astype(F32)
    sub = lax.broadcasted_iota(jnp.int32, (8, width), 0)
    lanes = lax.broadcasted_iota(jnp.int32, (8, width), 1)
    for k in range(0, width, 8):
        left, right = work[k : k + 8, :width], work[k : k + 8, width:]
        columns = [jnp.broadcast_to(left[:, k + j : k + j + 1], (8, width)) for j in range(8)]
        scale = jnp.zeros((8, width), F32)
        for j in range(8):
            pivot = jnp.broadcast_to(columns[j][j : j + 1, :], (8, width))
            root = lax.rsqrt(pivot)
            scale = jnp.where(sub == j, root, scale)
            if j < 7:
                ratio = jnp.where(sub > j, columns[j] / pivot, 0.0)
                left = left - ratio * jnp.broadcast_to(left[j : j + 1, :], (8, width))
                right = right - ratio * jnp.broadcast_to(right[j : j + 1, :], (8, width))
                for m in range(j + 1, 8):
                    columns[m] = columns[m] - ratio * jnp.broadcast_to(columns[m][j : j + 1, :], (8, width))
        left, right = left * scale, right * scale
        work[k : k + 8, :width] = left
        work[k : k + 8, width:] = right
        if k + 8 < width:
            coefficients = jnp.where(lanes >= k + 8, left, 0.0).T
            panel = jnp.concatenate([left, right], axis=1)
            update = jnp.dot(coefficients[k + 8 :], panel, precision=HIGHEST, preferred_element_type=F32)
            work[k + 8 :, :] -= update
    inverse = jnp.where(row >= lane, work[:, width:], 0.0)
    basis = jnp.dot(inverse, rows_ref[...], precision=HIGHEST, preferred_element_type=F32)
    if last is None:
        out_ref[...] = basis
        gram_out_ref[...] = lax.dot_general(
            basis, basis, (((1,), (1,)), ((), ())), precision=HIGHEST, preferred_element_type=F32
        )
    else:
        out_ref[...] = (basis * last).T
        gram_out_ref[...] = gram_ref[...]


def basis_of(gram, rows, last=None):
    width, snps = rows.shape
    shape = (width, snps) if last is None else (snps, width)
    return pl.pallas_call(
        functools.partial(basis_kernel, last),
        out_shape=(jax.ShapeDtypeStruct(shape, F32), jax.ShapeDtypeStruct((width, width), F32)),
        in_specs=[pl.BlockSpec(memory_space=pltpu.VMEM)] * 2,
        out_specs=[pl.BlockSpec(memory_space=pltpu.VMEM)] * 2,
        scratch_shapes=[pltpu.VMEM((width, 2 * width), F32)],
        name="basis",
    )(gram, rows)


def body(chroms, snps, genotypes, probes):
    plan = Plan(genotypes.shape[0], chroms, snps)
    rows, partial_gram = range_rows(plan, genotypes, probes)
    total_snps = rows.shape[1] * chroms * snps
    gram_first = lax.psum(partial_gram, AXES)
    range_log_norms = 0.1 * jnp.log(jnp.diagonal(gram_first) / total_snps)
    first_basis, partial_gram = basis_of(gram_first, rows)
    gram_second = lax.psum(partial_gram, AXES)
    unit_basis, _ = basis_of(gram_second, first_basis, math.sqrt(total_snps))
    return unit_basis, range_log_norms


def solution(mesh):
    return jax.shard_map(
        functools.partial(body, mesh.shape["chrom"], mesh.shape["snp"]),
        mesh=mesh,
        in_specs=(P(None, AXES), P(AXES, None)),
        out_specs=(P(AXES, None), P()),
        check_vma=False,
    )
```

time: 499 us -> 375 us (0.75)
  waiting for transfers between devices: 392 us -> 236 us
  Pallas kernels: 0 us -> 119 us
  other arithmetic: 64.7 us -> 0.53 us
  matrix products: 19.7 us -> 0 us
    psum x3 -> x2, waiting for transfers between devices: 392 us -> 236 us  [the longest x1 120 us: body(): gram_first = lax.psum(partial_gram, AXES)]
    pallas_call x0 -> x3, Pallas kernels: none -> 119 us  [the longest x1 99.8 us: range_rows(): pl.pallas_call(functools.partial(range_kernel, plan), out_shape=(jax.Shap...]
    another operation x10 -> x0, other arithmetic: 45.7 us -> none  [the longest x6 24.8 us: unit_columns(): lower_factor = jnp.linalg.cholesky(gram_matrix)]
    dot_general x4 -> x0, matrix products: 18.9 us -> none  [the longest x1 11.3 us: body(): lax.dot_general(scaled, sketch_parts, (((0,), (0,)), ((), ())), preferred...]
    reduce_sum x2 -> x0, other arithmetic: 11.5 us -> none  [the longest x1 7.93 us: standardize(): column_mean = jnp.mean(values, axis=0, keepdims=True)]
    convert_element_type x3 -> x0, other arithmetic: 5.26 us -> none  [the longest x1 3.16 us: split_parts(): sketch_high = lax.optimization_barrier(sketch.astype(jnp.bfloat16))]
  transfers between devices with their start and end apart: 3 -> 2, of which waited for: 3 -> 2; matrix products, arithmetic and copies ran while one was open for 0% -> 1% of each run, Pallas kernels for 0% -> 0%
where the time goes in v1:
time: 375 us; the launch traced here: 373 us
  waiting for transfers between devices  236 us (63%)
  Pallas kernels  119 us (32%)
  between operations  14.1 us (4%)
    psum x1, waiting for transfers between devices, body(): gram_first = lax.psum(partial_gram, AXES)  120 us
    psum x1, waiting for transfers between devices, body(): gram_second = lax.psum(partial_gram, AXES)  116 us
    pallas_call x1, Pallas kernels, range_rows(): pl.pallas_call(functools.partial(range_kernel, plan), out_shape=(jax.Shap...  99.8 us
    pallas_call x2, Pallas kernels, basis_of(): pl.pallas_call(functools.partial(basis_kernel, last), out_shape=(jax.Shap...  19.2 us
  transfers between devices with their start and end apart: 2, of which 2 were waited for; matrix products, arithmetic and copies ran while one was open for 1% of the time, Pallas kernels for 0%

profile of v1, /device:TPU:0, one launch (start us, length us, event | category | flops | bytes accessed | tf_op | source)
XLA Modules:
  0.0 373.5 jit_solution(3018686268506209974)
XLA Ops:
  7.2 0.0 all-reduce.3.cloned.1.call-start
  7.2 0.0 copy-start.1
  7.2 0.9 copy-done.1
  8.1 99.8 %range_rows.1 = (f32[128,512]{1,0:T(8,128)S(1)}, f32[128,128]{1,0:T(8,128)}) custom-call(bf16[12288,512]{1,0:T(8,128)(2,1)} %geno_hbm.1, bf16[512,128]{1,0:T(8,128)(2,1)S(1)} %copy-done.1), custom_call_target="tpu_custom_call" | custom-call | tf_op jit(solution)/shard_map/range_rows/pallas_call | solution.py:283
  107.9 0.0 copy-start
  107.9 0.7 copy-done
  108.6 0.0 all-reduce.3.cloned.1.call-update
  108.6 0.2 all-reduce.5.cloned.1.call-start
  108.8 120.1 %all-reduce.3.cloned.1.call-done.gram_ref = f32[128,128]{1,0:T(8,128)} async-done(((f32[128,128]{1,0:T(8,128)}), f32[128,128]{1,0:T(8,128)}) %all-reduce.3.cloned.1.call-update) | async-done | bytes 65552 | tf_op jit(solution)/shard_map/psum | solution.py:369
  229.0 9.7 %basis.2 = (f32[128,512]{1,0:T(8,128)}, f32[128,128]{1,0:T(8,128)}) custom-call(f32[128,128]{1,0:T(8,128)} %all-reduce.3.cloned.1.call-done.gram_ref, f32[128,512]{1,0:T(8,128)} %copy-done), custom_call_target="tpu_custom_call" | custom-call | tf_op jit(solution)/shard_map/basis/pallas_call | solution.py:355
  238.7 0.0 all-reduce.5.cloned.1.call-update
  238.7 1.9 gather_fusion
  240.6 0.5 log_multiply_fusion
  241.2 116.0 %all-reduce.5.cloned.1.call-done.gram_ref = f32[128,128]{1,0:T(8,128)} async-done(((f32[128,128]{1,0:T(8,128)}), f32[128,128]{1,0:T(8,128)}) %all-reduce.5.cloned.1.call-update) | async-done | bytes 65552 | tf_op jit(solution)/shard_map/psum | solution.py:372
  357.2 9.5 %basis.3 = (f32[512,128]{1,0:T(8,128)}, f32[128,128]{1,0:T(8,128)}) custom-call(f32[128,128]{1,0:T(8,128)} %all-reduce.5.cloned.1.call-done.gram_ref, f32[128,512]{1,0:T(8,128)} %get-tuple-element.10.rows_ref), custom_call_target="tpu_custom_call" | custom-call | tf_op jit(solution)/shard_map/basis/pallas_call | solution.py:355
  (1 shorter events, 0.0 us)
Async XLA Ops:
  7.2 221.8 %all-reduce.3.cloned.1.call-start = ((), (), s32[]{:S(2)}) async-start(), calls=%async_computation | async-start | bytes 131072 | tf_op jit(solution)/shard_map/psum | solution.py:369
  7.2 0.9 copy-start.1
  107.9 0.7 copy-start
  108.6 248.6 %all-reduce.5.cloned.1.call-start = ((), (), s32[]{:S(2)}) async-start(), calls=%async_computation.1 | async-start | bytes 131072 | tf_op jit(solution)/shard_map/psum | solution.py:372
Sparse Core Ops, SparseCore 0:
  108.7 120.1 all-reduce.2
  238.8 118.3 all-reduce.4

commit v2 on v1

--- a/solution.py
+++ b/solution.py
@@ -1,4 +1,5 @@
 import functools
+import itertools
 import math
 
 import jax
@@ -61,16 +62,100 @@
     )
 
 
-def greet(factors):
+def near_peer(plan, steps):
+    ids = {a: lax.axis_index(a) for a in AXES}
+    place = 0
+    for (axis, stride, size), step in zip(plan.near, steps):
+        mine = coordinate((axis, stride, size))
+        other = lax.rem(mine + step, size)
+        ids[axis] = ids[axis] + (other - mine) * stride
+        place = place * size + other
+    return tuple(ids[a] for a in AXES), place
+
+
+def greet(plan):
     barrier = pltpu.get_barrier_semaphore()
-    count = 0
-    for factor in factors:
-        for distance in range(1, factor[2]):
-            pl.semaphore_signal(
-                barrier, inc=1, device_id=peer_id(factor, distance), device_id_type=MESH
+    peers = [near_peer(plan, steps)[0] for steps in plan.near_steps]
+    for factor in plan.snp:
+        peers += [peer_id(factor, distance) for distance in range(1, factor[2])]
+    for peer in peers:
+        pl.semaphore_signal(barrier, inc=1, device_id=peer, device_id_type=MESH)
+    pl.semaphore_wait(barrier, len(peers))
+
+
+def sum_gram(plan, turn, gram, near, far, sems):
+    near_send, near_recv, far_send, far_recv, back_send, back_recv = sems
+    share = gram.shape[0] // plan.near_size
+    _, me = near_peer(plan, [0] * len(plan.near))
+    mine = rows_of(me * share, share)
+    copies = []
+    for i, steps in enumerate(plan.near_steps):
+        peer, place = near_peer(plan, steps)
+        copy = pltpu.make_async_remote_copy(
+            src_ref=gram.at[rows_of(place * share, share)],
+            dst_ref=near.at[turn, i],
+            send_sem=near_send.at[turn, i],
+            recv_sem=near_recv.at[turn, i],
+            device_id=peer,
+            device_id_type=MESH,
+        )
+        copy.start()
+        copies.append(copy)
+    value = gram[mine, :]
+    for i, copy in enumerate(copies):
+        copy.wait_recv()
+        value = value + near[turn, i]
+    pending = list(copies)
+    slot, first = 0, 0
+    for factor in plan.snp:
+        size = factor[2]
+        place = first + coordinate(factor)
+        far[turn, place] = value
+        copies = []
+        for distance in range(1, size):
+            copy = pltpu.make_async_remote_copy(
+                src_ref=far.at[turn, place],
+                dst_ref=far.at[turn, place],
+                send_sem=far_send.at[turn, slot],
+                recv_sem=far_recv.at[turn, slot],
+                device_id=peer_id(factor, distance),
+                device_id_type=MESH,
             )
-            count += 1
-    pl.semaphore_wait(barrier, count)
+            copy.start()
+            copies.append(copy)
+            slot += 1
+        for copy in copies:
+            copy.wait_recv()
+        value = far[turn, first]
+        for k in range(1, size):
+            value = value + far[turn, first + k]
+        first += size
+        pending += copies
+    for copy in pending:
+        copy.wait_send()
+    return value, me, share
+
+
+def spread_gram(plan, turn, value, me, share, total, sems):
+    mine = rows_of(me * share, share)
+    total[turn, mine, :] = value
+    copies = []
+    for i, steps in enumerate(plan.near_steps):
+        peer, _ = near_peer(plan, steps)
+        copy = pltpu.make_async_remote_copy(
+            src_ref=total.at[turn, mine],
+            dst_ref=total.at[turn, mine],
+            send_sem=sems[4].at[turn, i],
+            recv_sem=sems[5].at[turn, i],
+            device_id=peer,
+            device_id_type=MESH,
+        )
+        copy.start()
+        copies.append(copy)
+    for copy in copies:
+        copy.wait_recv()
+    for copy in copies:
+        copy.wait_send()
 
 
 def rows_of(start, rows):
@@ -85,21 +170,25 @@
     def __init__(self, samples, chroms, snps):
         self.devices = chroms * snps
         per_device = samples // self.devices
-        self.pieces = next(q for q in (8, 6, 4, 3, 2, 1) if per_device % (8 * q) == 0)
+        self.pieces = next(q for q in (16, 12, 8, 6, 4, 3, 2, 1) if per_device % (8 * q) == 0)
         self.rows = samples // self.pieces
         self.cores, self.chrom, self.snp = mesh_factors(chroms, snps)
         self.factors = self.cores + self.chrom + self.snp
         self.slots = sum(f[2] - 1 for f in self.factors)
+        self.lanes = max(1, len(self.chrom)) if self.pieces % max(1, len(self.chrom)) == 0 else 1
+        near = self.cores + [("chrom", 1, chroms)]
+        self.near = [f for f in near if f[2] > 1]
+        self.near_size = math.prod(f[2] for f in self.near)
+        self.near_steps = list(itertools.product(*[range(f[2]) for f in self.near]))[1:]
+        self.far_slots = sum(f[2] - 1 for f in self.snp)
+        self.far_size = sum(f[2] for f in self.snp)
 
     def order(self, piece):
         turn = piece % max(1, len(self.chrom))
         return self.cores + self.chrom[turn:] + self.chrom[:turn] + self.snp
 
-    def received(self):
-        return self.rows
-
-
-def range_kernel(plan, geno_hbm, probes_ref, range_ref, gram_ref, values, part, full, recv, acc, load_sem, rs_send, rs_recv, ag_send, ag_recv):
+
+def range_kernel(plan, geno_hbm, probes_ref, out_ref, norms_ref, values, part, full, recv, acc, gram, near, far, grams, work, load_sem, rs_send, rs_recv, ag_send, ag_recv, *sems):
     samples, snps = values.shape
     width = probes_ref.shape[1]
     rows, pieces = plan.rows, plan.pieces
@@ -109,7 +198,7 @@
         load = pltpu.make_async_copy(geno_hbm.at[piece], values.at[piece], load_sem.at[q])
         load.start()
         loads.append(load)
-    greet(plan.factors)
+    greet(plan)
 
     block = math.gcd(rows, 512)
     zero = jnp.zeros((16, snps), F32)
@@ -261,30 +350,86 @@
             gather_end(q, 0)
             project(q)
 
-    for time in range(pieces + 2 * stages):
+    lanes = plan.lanes
+    for time in range(pieces // lanes + 2 * stages):
         for q in range(pieces):
-            if 0 <= time - q <= 2 * stages:
-                step(q, time - q)
+            if 0 <= time - q // lanes <= 2 * stages:
+                step(q, time - q // lanes)
     for sent in copies.values():
         for copy in sent:
             copy.wait_send()
 
     result = acc[:width] + acc[width : 2 * width] + acc[2 * width :]
-    range_ref[...] = result
-    gram_ref[...] = lax.dot_general(
-        result, result, (((1,), (1,)), ((), ())), precision=HIGHEST, preferred_element_type=F32
-    )
-
-
-def range_rows(plan, genotypes, probes):
+    total_snps = snps * plan.devices
+    for turn in range(2):
+        gram[turn] = lax.dot_general(
+            result, result, (((1,), (1,)), ((), ())), precision=HIGHEST, preferred_element_type=F32
+        )
+        value, me, share = sum_gram(plan, turn, gram.at[turn], near, far, sems)
+        spread_gram(plan, turn, value, me, share, grams, sems)
+        total_gram = grams[turn]
+        if turn == 0:
+            row = lax.broadcasted_iota(jnp.int32, (width, width), 0)
+            lane = lax.broadcasted_iota(jnp.int32, (width, width), 1)
+            diagonal = jnp.sum(jnp.where(row == lane, total_gram, 0.0), axis=0, keepdims=True)
+            norms_ref[...] = 0.1 * jnp.log(diagonal / total_snps)
+        inverse = inverse_factor(total_gram, work)
+        result = jnp.dot(inverse, result, precision=HIGHEST, preferred_element_type=F32)
+    out_ref[...] = (result * math.sqrt(total_snps)).T
+
+
+PANEL = 16
+
+
+def inverse_factor(gram, work):
+    width = gram.shape[0]
+    row = lax.broadcasted_iota(jnp.int32, (width, width), 0)
+    lane = lax.broadcasted_iota(jnp.int32, (width, width), 1)
+    work[:, :width] = gram
+    work[:, width:] = jnp.where(row == lane, 1.0, 0.0).astype(F32)
+    shape = (PANEL, width)
+    sub = lax.broadcasted_iota(jnp.int32, shape, 0)
+    lanes = lax.broadcasted_iota(jnp.int32, shape, 1)
+
+    def of_row(array, j):
+        return jnp.broadcast_to(array[j : j + 1, :], shape)
+
+    for k in range(0, width, PANEL):
+        left, right = work[k : k + PANEL, :width], work[k : k + PANEL, width:]
+        columns = [jnp.broadcast_to(left[:, k + j : k + j + 1], shape) for j in range(PANEL)]
+        scale = jnp.zeros(shape, F32)
+        for j in range(PANEL):
+            root = lax.rsqrt(of_row(columns[j], j))
+            scale = jnp.where(sub == j, root, scale)
+            if j < PANEL - 1:
+                ratio = jnp.where(sub > j, columns[j] * (root * root), 0.0)
+                for m in range(j + 1, PANEL):
+                    columns[m] = columns[m] - ratio * of_row(columns[m], j)
+                left = left - ratio * of_row(left, j)
+                right = right - ratio * of_row(right, j)
+        left, right = left * scale, right * scale
+        work[k : k + PANEL, width:] = right
+        if k + PANEL < width:
+            coefficients = jnp.where(lanes >= k + PANEL, left, 0.0).T
+            panel = jnp.concatenate([left, right], axis=1)
+            work[k + PANEL :, :] -= jnp.dot(
+                coefficients[k + PANEL :], panel, precision=HIGHEST, preferred_element_type=F32
+            )
+    return jnp.where(row >= lane, work[:, width:], 0.0)
+
+
+def range_basis(plan, genotypes, probes):
     samples, snps = genotypes.shape
     width = probes.shape[1]
     slots = max(1, plan.slots)
+    near = max(1, len(plan.near_steps))
+    share = width // plan.near_size
+    dma = pltpu.SemaphoreType.DMA
     return pl.pallas_call(
         functools.partial(range_kernel, plan),
         out_shape=(
-            jax.ShapeDtypeStruct((width, snps), F32),
-            jax.ShapeDtypeStruct((width, width), F32),
+            jax.ShapeDtypeStruct((snps, width), F32),
+            jax.ShapeDtypeStruct((1, width), F32),
         ),
         in_specs=[pl.BlockSpec(memory_space=pl.ANY), pl.BlockSpec(memory_space=pltpu.VMEM)],
         out_specs=[pl.BlockSpec(memory_space=pltpu.VMEM)] * 2,
@@ -294,84 +439,28 @@
             pltpu.VMEM((samples, width), F32),
             pltpu.VMEM((plan.pieces, plan.rows, width), F32),
             pltpu.VMEM((3 * width, snps), F32),
-            pltpu.SemaphoreType.DMA((plan.pieces,)),
-            pltpu.SemaphoreType.DMA((plan.pieces, slots)),
-            pltpu.SemaphoreType.DMA((plan.pieces, slots)),
-            pltpu.SemaphoreType.DMA((plan.pieces, slots)),
-            pltpu.SemaphoreType.DMA((plan.pieces, slots)),
-        ],
+            pltpu.VMEM((2, width, width), F32),
+            pltpu.VMEM((2, near, share, width), F32),
+            pltpu.VMEM((2, max(1, plan.far_size), share, width), F32),
+            pltpu.VMEM((2, width, width), F32),
+            pltpu.VMEM((width, 2 * width), F32),
+            dma((plan.pieces,)),
+        ]
+        + [dma((plan.pieces, slots))] * 4
+        + [dma((2, near))] * 2
+        + [dma((2, max(1, plan.far_slots)))] * 2
+        + [dma((2, near))] * 2,
         compiler_params=pltpu.CompilerParams(
             collective_id=0, has_side_effects=True, vmem_limit_bytes=48 * 1024 * 1024
         ),
-        name="range_rows",
+        name="range_basis",
     )(genotypes, probes)
-
-
-def basis_kernel(last, gram_ref, rows_ref, out_ref, gram_out_ref, work):
-    width = gram_ref.shape[0]
-    row = lax.broadcasted_iota(jnp.int32, (width, width), 0)
-    lane = lax.broadcasted_iota(jnp.int32, (width, width), 1)
-    work[:, :width] = gram_ref[...]
-    work[:, width:] = jnp.where(row == lane, 1.0, 0.0).astype(F32)
-    sub = lax.broadcasted_iota(jnp.int32, (8, width), 0)
-    lanes = lax.broadcasted_iota(jnp.int32, (8, width), 1)
-    for k in range(0, width, 8):
-        left, right = work[k : k + 8, :width], work[k : k + 8, width:]
-        columns = [jnp.broadcast_to(left[:, k + j : k + j + 1], (8, width)) for j in range(8)]
-        scale = jnp.zeros((8, width), F32)
-        for j in range(8):
-            pivot = jnp.broadcast_to(columns[j][j : j + 1, :], (8, width))
-            root = lax.rsqrt(pivot)
-            scale = jnp.where(sub == j, root, scale)
-            if j < 7:
-                ratio = jnp.where(sub > j, columns[j] / pivot, 0.0)
-                left = left - ratio * jnp.broadcast_to(left[j : j + 1, :], (8, width))
-                right = right - ratio * jnp.broadcast_to(right[j : j + 1, :], (8, width))
-                for m in range(j + 1, 8):
-                    columns[m] = columns[m] - ratio * jnp.broadcast_to(columns[m][j : j + 1, :], (8, width))
-        left, right = left * scale, right * scale
-        work[k : k + 8, :width] = left
-        work[k : k + 8, width:] = right
-        if k + 8 < width:
-            coefficients = jnp.where(lanes >= k + 8, left, 0.0).T
-            panel = jnp.concatenate([left, right], axis=1)
-            update = jnp.dot(coefficients[k + 8 :], panel, precision=HIGHEST, preferred_element_type=F32)
-            work[k + 8 :, :] -= update
-    inverse = jnp.where(row >= lane, work[:, width:], 0.0)
-    basis = jnp.dot(inverse, rows_ref[...], precision=HIGHEST, preferred_element_type=F32)
-    if last is None:
-        out_ref[...] = basis
-        gram_out_ref[...] = lax.dot_general(
-            basis, basis, (((1,), (1,)), ((), ())), precision=HIGHEST, preferred_element_type=F32
-        )
-    else:
-        out_ref[...] = (basis * last).T
-        gram_out_ref[...] = gram_ref[...]
-
-
-def basis_of(gram, rows, last=None):
-    width, snps = rows.shape
-    shape = (width, snps) if last is None else (snps, width)
-    return pl.pallas_call(
-        functools.partial(basis_kernel, last),
-        out_shape=(jax.ShapeDtypeStruct(shape, F32), jax.ShapeDtypeStruct((width, width), F32)),
-        in_specs=[pl.BlockSpec(memory_space=pltpu.VMEM)] * 2,
-        out_specs=[pl.BlockSpec(memory_space=pltpu.VMEM)] * 2,
-        scratch_shapes=[pltpu.VMEM((width, 2 * width), F32)],
-        name="basis",
-    )(gram, rows)
 
 
 def body(chroms, snps, genotypes, probes):
     plan = Plan(genotypes.shape[0], chroms, snps)
-    rows, partial_gram = range_rows(plan, genotypes, probes)
-    total_snps = rows.shape[1] * chroms * snps
-    gram_first = lax.psum(partial_gram, AXES)
-    range_log_norms = 0.1 * jnp.log(jnp.diagonal(gram_first) / total_snps)
-    first_basis, partial_gram = basis_of(gram_first, rows)
-    gram_second = lax.psum(partial_gram, AXES)
-    unit_basis, _ = basis_of(gram_second, first_basis, math.sqrt(total_snps))
-    return unit_basis, range_log_norms
+    unit_basis, norms = range_basis(plan, genotypes, probes)
+    return unit_basis, norms.reshape(-1)
 
 
 def solution(mesh):

time: 375 us -> 116 us (0.31)
  waiting for transfers between devices: 236 us -> 0 us
  between operations: 14.1 us -> 0.65 us
  Pallas kernels: 119 us -> 113 us
    psum x2 -> x0, waiting for transfers between devices: 236 us -> none  [the longest x1 120 us: body(): gram_first = lax.psum(partial_gram, AXES)]
    pallas_call x3 -> x1, Pallas kernels: 119 us -> 113 us  [range_basis(): pl.pallas_call(functools.partial(range_kernel, plan), out_shape=(jax.Shap...]
  transfers between devices with their start and end apart: 2 -> 0, of which waited for: 2 -> 0; matrix products, arithmetic and copies ran while one was open for 1% -> 0% of each run, Pallas kernels for 0% -> 0%
where the time goes in v2:
time: 116 us; the launch traced here: 115 us
  Pallas kernels  113 us (97%)
  local copies, waits for them, and re-layouts  2.11 us (2%)
    pallas_call x1, Pallas kernels, range_basis(): pl.pallas_call(functools.partial(range_kernel, plan), out_shape=(jax.Shap...  113 us

profile of v2, /device:TPU:0, one launch (start us, length us, event | category | flops | bytes accessed | tf_op | source)
XLA Modules:
  0.0 115.4 jit_solution(8930406795990300333)
XLA Ops:
  0.6 0.0 copy-start
  0.6 0.9 copy-done
  1.5 112.6 %range_basis.1 = (f32[512,128]{1,0:T(8,128)S(1)}, f32[1,128]{1,0:T(1,128)S(1)}) custom-call(bf16[12288,512]{1,0:T(8,128)(2,1)} %geno_hbm.1, bf16[512,128]{1,0:T(8,128)(2,1)S(1)} %copy-done), custom_call_target="tpu_custom_call" | custom-call | tf_op jit(solution)/shard_map/range_basis/pallas_call | solution.py:428
  114.2 0.7 copy.6
  114.9 0.5 copy.7
Async XLA Ops:
  0.6 0.9 copy-start

commit v3 on v2

--- a/solution.py
+++ b/solution.py
@@ -45,6 +45,52 @@
     snp = [(a, s * core, n) for a, s, n in axis_factors("snp", split_size(snps // core))]
     cores = [("snp", 1, core)] if core > 1 else []
     return cores, chrom, snp
+
+
+LINK = {"core": 600e3, "far": 50e3}
+DELAY = 2.0
+
+
+def schedule(plan, row_bytes):
+    stages = len(plan.factors)
+    last = 2 * stages
+    free, ready, at, order = {}, {}, [0] * plan.pieces, []
+    shares = []
+    for q in range(plan.pieces):
+        size, path = plan.rows, []
+        for factor in plan.order(q):
+            size //= factor[2]
+            path.append((factor, size))
+        shares.append(path)
+        ready[q] = 0.0
+    now = 0.0
+    while any(t <= last for t in at):
+        open_ = [q for q in range(plan.pieces) if at[q] <= last]
+        there = [q for q in open_ if ready[q] <= now]
+        if there:
+            q = max(there, key=lambda q: (at[q] != last, at[q], -q))
+        else:
+            q = min(open_, key=lambda q: (ready[q], q))
+        t = at[q]
+        if t == 0:
+            work = plan.rows * 0.5e-3
+        elif t == last:
+            work = plan.rows * 0.65e-3
+        elif t <= stages:
+            work = 0.15 + shares[q][t - 1][1] * row_bytes * 0.2e-6
+        else:
+            work = 0.1
+        now = max(now, ready[q]) + work
+        order.append((q, t))
+        at[q] = t + 1
+        if t < last:
+            factor, share = shares[q][t if t < stages else last - 1 - t]
+            core = factor in plan.cores
+            link = "snp" if factor in plan.snp else factor
+            load = factor[2] ** 2 / 4 * share * row_bytes / LINK["core" if core else "far"]
+            free[link] = max(now, free.get(link, 0.0)) + load
+            ready[q] = free[link] + DELAY
+    return order
 
 
 def coordinate(factor):
@@ -170,12 +216,11 @@
     def __init__(self, samples, chroms, snps):
         self.devices = chroms * snps
         per_device = samples // self.devices
-        self.pieces = next(q for q in (16, 12, 8, 6, 4, 3, 2, 1) if per_device % (8 * q) == 0)
+        self.pieces = next(q for q in (24, 16, 12, 8, 6, 4, 3, 2, 1) if per_device % (8 * q) == 0)
         self.rows = samples // self.pieces
         self.cores, self.chrom, self.snp = mesh_factors(chroms, snps)
         self.factors = self.cores + self.chrom + self.snp
         self.slots = sum(f[2] - 1 for f in self.factors)
-        self.lanes = max(1, len(self.chrom)) if self.pieces % max(1, len(self.chrom)) == 0 else 1
         near = self.cores + [("chrom", 1, chroms)]
         self.near = [f for f in near if f[2] > 1]
         self.near_size = math.prod(f[2] for f in self.near)
@@ -188,7 +233,7 @@
         return self.cores + self.chrom[turn:] + self.chrom[:turn] + self.snp
 
 
-def range_kernel(plan, geno_hbm, probes_ref, out_ref, norms_ref, values, part, full, recv, acc, gram, near, far, grams, work, load_sem, rs_send, rs_recv, ag_send, ag_recv, *sems):
+def range_kernel(plan, geno_hbm, probes_hbm, out_ref, norms_ref, values, probes_ref, part, full, recv, acc, gram, near, far, grams, work, load_sem, probe_sem, rs_send, rs_recv, ag_send, ag_recv, *sems):
     samples, snps = values.shape
     width = probes_ref.shape[1]
     rows, pieces = plan.rows, plan.pieces
@@ -198,6 +243,8 @@
         load = pltpu.make_async_copy(geno_hbm.at[piece], values.at[piece], load_sem.at[q])
         load.start()
         loads.append(load)
+    probe_load = pltpu.make_async_copy(probes_hbm, probes_ref, probe_sem)
+    probe_load.start()
     greet(plan)
 
     block = math.gcd(rows, 512)
@@ -224,6 +271,7 @@
     whole, square = total.astype(jnp.int32), squares.astype(jnp.int32)
     spread = (square * samples - whole * whole).astype(F32) / float(samples) ** 2
     factor = lax.rsqrt(jnp.sqrt(jnp.sqrt(spread + 1e-05)))
+    probe_load.wait()
     probes = probes_ref[...]
     acc[...] = jnp.zeros_like(acc)
 
@@ -314,7 +362,7 @@
         for copy in copies["ag", q, s]:
             copy.wait_recv()
 
-    depth = math.gcd(rows, 768)
+    depth = block_of(rows, 768)
 
     def project(q):
         def one(i, _):
@@ -350,11 +398,8 @@
             gather_end(q, 0)
             project(q)
 
-    lanes = plan.lanes
-    for time in range(pieces // lanes + 2 * stages):
-        for q in range(pieces):
-            if 0 <= time - q // lanes <= 2 * stages:
-                step(q, time - q // lanes)
+    for q, t in schedule(plan, width * 4):
+        step(q, t)
     for sent in copies.values():
         for copy in sent:
             copy.wait_send()
@@ -387,6 +432,7 @@
     lane = lax.broadcasted_iota(jnp.int32, (width, width), 1)
     work[:, :width] = gram
     work[:, width:] = jnp.where(row == lane, 1.0, 0.0).astype(F32)
+    following = work[:PANEL, :]
     shape = (PANEL, width)
     sub = lax.broadcasted_iota(jnp.int32, shape, 0)
     lanes = lax.broadcasted_iota(jnp.int32, shape, 1)
@@ -395,7 +441,7 @@
         return jnp.broadcast_to(array[j : j + 1, :], shape)
 
     for k in range(0, width, PANEL):
-        left, right = work[k : k + PANEL, :width], work[k : k + PANEL, width:]
+        left, right = following[:, :width], following[:, width:]
         columns = [jnp.broadcast_to(left[:, k + j : k + j + 1], shape) for j in range(PANEL)]
         scale = jnp.zeros(shape, F32)
         for j in range(PANEL):
@@ -412,9 +458,14 @@
         if k + PANEL < width:
             coefficients = jnp.where(lanes >= k + PANEL, left, 0.0).T
             panel = jnp.concatenate([left, right], axis=1)
-            work[k + PANEL :, :] -= jnp.dot(
-                coefficients[k + PANEL :], panel, precision=HIGHEST, preferred_element_type=F32
+            cut = k + 2 * PANEL
+            following = work[k + PANEL : cut, :] - jnp.dot(
+                coefficients[k + PANEL : cut], panel, precision=HIGHEST, preferred_element_type=F32
             )
+            if cut < width:
+                work[cut:, :] -= jnp.dot(
+                    coefficients[cut:], panel, precision=HIGHEST, preferred_element_type=F32
+                )
     return jnp.where(row >= lane, work[:, width:], 0.0)
 
 
@@ -431,10 +482,11 @@
             jax.ShapeDtypeStruct((snps, width), F32),
             jax.ShapeDtypeStruct((1, width), F32),
         ),
-        in_specs=[pl.BlockSpec(memory_space=pl.ANY), pl.BlockSpec(memory_space=pltpu.VMEM)],
+        in_specs=[pl.BlockSpec(memory_space=pl.ANY)] * 2,
         out_specs=[pl.BlockSpec(memory_space=pltpu.VMEM)] * 2,
         scratch_shapes=[
             pltpu.VMEM((samples, snps), BF16),
+            pltpu.VMEM((snps, width), BF16),
             pltpu.VMEM((samples, width), F32),
             pltpu.VMEM((samples, width), F32),
             pltpu.VMEM((plan.pieces, plan.rows, width), F32),
@@ -445,6 +497,7 @@
             pltpu.VMEM((2, width, width), F32),
             pltpu.VMEM((width, 2 * width), F32),
             dma((plan.pieces,)),
+            dma(()),
         ]
         + [dma((plan.pieces, slots))] * 4
         + [dma((2, near))] * 2

time: 116 us -> 112 us (0.966)
  Pallas kernels: 113 us -> 109 us
    pallas_call x1, Pallas kernels: 113 us -> 109 us  [range_basis(): pl.pallas_call(functools.partial(range_kernel, plan), out_shape=(jax.Shap...]
where the time goes in v3:
time: 112 us
  Pallas kernels  109 us (97%)
  local copies, waits for them, and re-layouts  2.11 us (2%)
    pallas_call x1, Pallas kernels, range_basis(): pl.pallas_call(functools.partial(range_kernel, plan), out_shape=(jax.Shap...  109 us

profile of v3, /device:TPU:0, one launch (start us, length us, event | category | flops | bytes accessed | tf_op | source)
XLA Modules:
  0.0 111.7 jit_solution(5128186973265963491)
XLA Ops:
  0.6 0.0 copy-start
  0.6 0.9 copy-done
  1.5 109.0 %range_basis.1 = (f32[512,128]{1,0:T(8,128)S(1)}, f32[1,128]{1,0:T(1,128)S(1)}) custom-call(bf16[12288,512]{1,0:T(8,128)(2,1)} %geno_hbm.1, bf16[512,128]{1,0:T(8,128)(2,1)S(1)} %copy-done), custom_call_target="tpu_custom_call" | custom-call | tf_op jit(solution)/shard_map/range_basis/pallas_call | solution.py:479
  110.5 0.7 copy.6
  111.2 0.5 copy.7
Async XLA Ops:
  0.6 0.9 copy-start

commit v4 on v3

--- a/solution.py
+++ b/solution.py
@@ -177,9 +177,7 @@
             value = value + far[turn, first + k]
         first += size
         pending += copies
-    for copy in pending:
-        copy.wait_send()
-    return value, me, share
+    return value, me, share, pending
 
 
 def spread_gram(plan, turn, value, me, share, total, sems):
@@ -200,8 +198,7 @@
         copies.append(copy)
     for copy in copies:
         copy.wait_recv()
-    for copy in copies:
-        copy.wait_send()
+    return copies
 
 
 def rows_of(start, rows):
@@ -400,9 +397,7 @@
 
     for q, t in schedule(plan, width * 4):
         step(q, t)
-    for sent in copies.values():
-        for copy in sent:
-            copy.wait_send()
+    pending = [copy for sent in copies.values() for copy in sent]
 
     result = acc[:width] + acc[width : 2 * width] + acc[2 * width :]
     total_snps = snps * plan.devices
@@ -410,8 +405,8 @@
         gram[turn] = lax.dot_general(
             result, result, (((1,), (1,)), ((), ())), precision=HIGHEST, preferred_element_type=F32
         )
-        value, me, share = sum_gram(plan, turn, gram.at[turn], near, far, sems)
-        spread_gram(plan, turn, value, me, share, grams, sems)
+        value, me, share, sent = sum_gram(plan, turn, gram.at[turn], near, far, sems)
+        pending += sent + spread_gram(plan, turn, value, me, share, grams, sems)
         total_gram = grams[turn]
         if turn == 0:
             row = lax.broadcasted_iota(jnp.int32, (width, width), 0)
@@ -421,9 +416,18 @@
         inverse = inverse_factor(total_gram, work)
         result = jnp.dot(inverse, result, precision=HIGHEST, preferred_element_type=F32)
     out_ref[...] = (result * math.sqrt(total_snps)).T
+    for copy in pending:
+        copy.wait_send()
 
 
 PANEL = 16
+
+
+def three_parts(array):
+    high = array.astype(BF16).astype(F32)
+    rest = array - high
+    mid = rest.astype(BF16).astype(F32)
+    return high, mid, rest - mid
 
 
 def inverse_factor(gram, work):
@@ -448,24 +452,25 @@
             root = lax.rsqrt(of_row(columns[j], j))
             scale = jnp.where(sub == j, root, scale)
             if j < PANEL - 1:
-                ratio = jnp.where(sub > j, columns[j] * (root * root), 0.0)
+                ratio = columns[j] * (root * root)
                 for m in range(j + 1, PANEL):
                     columns[m] = columns[m] - ratio * of_row(columns[m], j)
-                left = left - ratio * of_row(left, j)
-                right = right - ratio * of_row(right, j)
+                below = jnp.where(sub > j, ratio, 0.0)
+                left = left - below * of_row(left, j)
+                right = right - below * of_row(right, j)
         left, right = left * scale, right * scale
         work[k : k + PANEL, width:] = right
         if k + PANEL < width:
-            coefficients = jnp.where(lanes >= k + PANEL, left, 0.0).T
-            panel = jnp.concatenate([left, right], axis=1)
             cut = k + 2 * PANEL
+            high, mid, low = three_parts(jnp.where(lanes >= k + PANEL, left, 0.0))
+            factors = jnp.concatenate([high, high, mid, high, low, mid], axis=0).T.astype(BF16)
+            high, mid, low = three_parts(jnp.concatenate([left, right], axis=1))
+            panel = jnp.concatenate([high, mid, high, low, high, mid], axis=0).astype(BF16)
             following = work[k + PANEL : cut, :] - jnp.dot(
-                coefficients[k + PANEL : cut], panel, precision=HIGHEST, preferred_element_type=F32
+                factors[k + PANEL : cut], panel, preferred_element_type=F32
             )
             if cut < width:
-                work[cut:, :] -= jnp.dot(
-                    coefficients[cut:], panel, precision=HIGHEST, preferred_element_type=F32
-                )
+                work[cut:, :] -= jnp.dot(factors[cut:], panel, preferred_element_type=F32)
     return jnp.where(row >= lane, work[:, width:], 0.0)
 
 
@@ -504,7 +509,7 @@
         + [dma((2, max(1, plan.far_slots)))] * 2
         + [dma((2, near))] * 2,
         compiler_params=pltpu.CompilerParams(
-            collective_id=0, has_side_effects=True, vmem_limit_bytes=48 * 1024 * 1024
+            collective_id=0, has_side_effects=True, vmem_limit_bytes=63 * 1024 * 1024
         ),
         name="range_basis",
     )(genotypes, probes)

time: 112 us -> 113 us (level)
    unnamed x4 -> x2, local copies, waits for them, and re-layouts: 2.11 us -> 2.8 us
where the time goes in v4:
time: 113 us; the launch traced here: 112 us
  Pallas kernels  109 us (96%)
  local copies, waits for them, and re-layouts  2.8 us (2%)
    pallas_call x1, Pallas kernels, range_basis(): pl.pallas_call(functools.partial(range_kernel, plan), out_shape=(jax.Shap...  109 us
    unnamed x2, local copies, waits for them, and re-layouts  2.8 us

profile of v4, /device:TPU:0, one launch (start us, length us, event | category | flops | bytes accessed | tf_op | source)
XLA Modules:
  0.0 112.4 jit_solution(17890953199060792682)
XLA Ops:
  0.6 109.0 %range_basis.1 = (f32[512,128]{1,0:T(8,128)}, f32[1,128]{1,0:T(1,128)}) custom-call(bf16[12288,512]{1,0:T(8,128)(2,1)} %geno_hbm.1, bf16[512,128]{1,0:T(8,128)(2,1)} %probes_hbm.1), custom_call_target="tpu_custom_call" | custom-call | tf_op jit(solution)/shard_map/range_basis/pallas_call | solution.py:484
  109.6 1.7 %copy.6 = f32[512,128]{1,0:T(8,128)} copy(f32[512,128]{1,0:T(8,128)} %get-tuple-element.8) | data formatting | bytes 524288
  111.3 1.1 %copy.7 = f32[128]{0:T(128)} copy(f32[128]{0:T(128)} %bitcast.1) | data formatting | bytes 1024

commit v5 on v4

--- a/solution.py
+++ b/solution.py
@@ -48,7 +48,7 @@
 
 
 LINK = {"core": 600e3, "far": 50e3}
-DELAY = 2.0
+DELAY = 1.5
 
 
 def schedule(plan, row_bytes):
@@ -213,7 +213,7 @@
     def __init__(self, samples, chroms, snps):
         self.devices = chroms * snps
         per_device = samples // self.devices
-        self.pieces = next(q for q in (24, 16, 12, 8, 6, 4, 3, 2, 1) if per_device % (8 * q) == 0)
+        self.pieces = next(q for q in (16, 12, 8, 6, 4, 3, 2, 1) if per_device % (8 * q) == 0)
         self.rows = samples // self.pieces
         self.cores, self.chrom, self.snp = mesh_factors(chroms, snps)
         self.factors = self.cores + self.chrom + self.snp
@@ -509,7 +509,7 @@
         + [dma((2, max(1, plan.far_slots)))] * 2
         + [dma((2, near))] * 2,
         compiler_params=pltpu.CompilerParams(
-            collective_id=0, has_side_effects=True, vmem_limit_bytes=63 * 1024 * 1024
+            collective_id=0, has_side_effects=True, vmem_limit_bytes=48 * 1024 * 1024
         ),
         name="range_basis",
     )(genotypes, probes)

time: 113 us -> 115 us (1.018)
  Pallas kernels: 109 us -> 112 us
    pallas_call x1, Pallas kernels: 109 us -> 112 us  [range_basis(): pl.pallas_call(functools.partial(range_kernel, plan), out_shape=(jax.Shap...]
    unnamed x2 -> x4, local copies, waits for them, and re-layouts: 2.8 us -> 2.11 us
where the time goes in v5:
time: 115 us
  Pallas kernels  112 us (97%)
  local copies, waits for them, and re-layouts  2.11 us (2%)
    pallas_call x1, Pallas kernels, range_basis(): pl.pallas_call(functools.partial(range_kernel, plan), out_shape=(jax.Shap...  112 us

profile of v5, /device:TPU:0, one launch (start us, length us, event | category | flops | bytes accessed | tf_op | source)
XLA Modules:
  0.0 115.0 jit_solution(13067634538466534709)
XLA Ops:
  0.6 0.0 copy-start
  0.6 0.9 copy-done
  1.5 112.2 %range_basis.1 = (f32[512,128]{1,0:T(8,128)S(1)}, f32[1,128]{1,0:T(1,128)S(1)}) custom-call(bf16[12288,512]{1,0:T(8,128)(2,1)} %geno_hbm.1, bf16[512,128]{1,0:T(8,128)(2,1)S(1)} %copy-done), custom_call_target="tpu_custom_call" | custom-call | tf_op jit(solution)/shard_map/range_basis/pallas_call | solution.py:484
  113.7 0.7 copy.6
  114.5 0.5 copy.7
Async XLA Ops:
  0.6 0.9 copy-start

commit v6 on v5

--- a/solution.py
+++ b/solution.py
@@ -47,8 +47,8 @@
     return cores, chrom, snp
 
 
-LINK = {"core": 600e3, "far": 50e3}
-DELAY = 1.5
+LINK = {"core": 100e3, "far": 50e3}
+DELAY = 1.0
 
 
 def schedule(plan, row_bytes):
@@ -213,7 +213,7 @@
     def __init__(self, samples, chroms, snps):
         self.devices = chroms * snps
         per_device = samples // self.devices
-        self.pieces = next(q for q in (16, 12, 8, 6, 4, 3, 2, 1) if per_device % (8 * q) == 0)
+        self.pieces = next(q for q in (24, 16, 12, 8, 6, 4, 3, 2, 1) if per_device % (8 * q) == 0)
         self.rows = samples // self.pieces
         self.cores, self.chrom, self.snp = mesh_factors(chroms, snps)
         self.factors = self.cores + self.chrom + self.snp

time: 115 us -> 134 us (1.17)
  Pallas kernels: 112 us -> 131 us
    pallas_call x1, Pallas kernels: 112 us -> 131 us  [range_basis(): pl.pallas_call(functools.partial(range_kernel, plan), out_shape=(jax.Shap...]
where the time goes in v6:
time: 134 us
  Pallas kernels  131 us (98%)
  local copies, waits for them, and re-layouts  2.11 us (2%)
    pallas_call x1, Pallas kernels, range_basis(): pl.pallas_call(functools.partial(range_kernel, plan), out_shape=(jax.Shap...  131 us

profile of v6, /device:TPU:0, one launch (start us, length us, event | category | flops | bytes accessed | tf_op | source)
XLA Modules:
  0.0 134.0 jit_solution(9837732442694088718)
XLA Ops:
  0.6 0.0 copy-start
  0.6 0.9 copy-done
  1.5 131.2 %range_basis.1 = (f32[512,128]{1,0:T(8,128)S(1)}, f32[1,128]{1,0:T(1,128)S(1)}) custom-call(bf16[12288,512]{1,0:T(8,128)(2,1)} %geno_hbm.1, bf16[512,128]{1,0:T(8,128)(2,1)S(1)} %copy-done), custom_call_target="tpu_custom_call" | custom-call | tf_op jit(solution)/shard_map/range_basis/pallas_call | solution.py:484
  132.8 0.7 copy.6
  133.5 0.5 copy.7
Async XLA Ops:
  0.6 0.9 copy-start
